TPU v7x, 512 devices: a whole 4x8x8 slice. The times are simulated.
512 devices in a mesh: gx: 8 (over y), gy: 16 (over z, x_lo), gz: 4 (over x_hi, core).
Axes of the slice: x: 4 (x_hi: 2, x_lo: 2; x = x_hi * 2 + x_lo), y: 8, z: 8, core: 2. Of those that a mesh axis runs over, the one named last changes fastest.
Arguments:
- pops: float32 [27, 16, 128, 1024], P(None, 'gz', 'gy', 'gx')
- solid: int32 [16, 128, 1024], P('gz', 'gy', 'gx'), may hold values from 0 to 1, as said below
- profile_table: float32 [8, 16], P(None, 'gz'), as said below
- profile_index: int32 [128], P('gy'), may hold values from 0 to 7
Outputs:
- updated: float32 [27, 16, 128, 1024], P(None, 'gz', 'gy', 'gx')
Inputs may be any that keep to these rules, and one draw needn't show every extreme that they name: `solid`: buildings are vertical columns on footprints of 4 x 4 cells aligned to multiples of 4; every cell with z index 15 is 0. `profile_table`: every profile's speeds lie in a band of positive values.
All inputs are finite; a program needn't handle non-finite values.
Results may differ from a plain program's by a relative error of at most 0.0003.
Values sent between devices are 32-bit elements; how exact they have to be, the bound alone decides.
A program may use at most 64 MiB of HBM per device.

v0:
```python
import jax
import jax.numpy as jnp
import numpy as np
from jax import lax
from jax.sharding import PartitionSpec as P

STEPS = 2
SPONGE = 32


tau_base = 0.52
smag_const = 0.17
root_two = 1.4142135623730951


def padded_2(array, sides, width):
    for axis, dim in sides:
        size, length = (lax.axis_size(axis), array.shape[dim])
        up = [(i, (i + 1) % size) for i in range(size)]
        down = [(j, i) for i, j in up]
        last = lax.slice_in_dim(array, length - width, length, axis=dim)
        initial = lax.slice_in_dim(array, 0, width, axis=dim)
        before = lax.ppermute(last, axis, up)
        after = lax.ppermute(initial, axis, down)
        array = jnp.concatenate([before, array, after], axis=dim)
    return array


def lattice():
    velocity = np.array(
        [[cx, cy, cz] for cz in (-1, 0, 1) for cy in (-1, 0, 1) for cx in (-1, 0, 1)]
    )
    lengths_sq = (velocity * velocity).sum(1)
    weights = np.array([8.0 / 27.0, 2.0 / 27.0, 1.0 / 54.0, 1.0 / 216.0])[lengths_sq]
    return (velocity, weights)


def mirror_of(number):
    velocity, weights = lattice()
    cx, cy, cz = velocity[number]
    return int((1 - cz) * 9 + (cy + 1) * 3 + (cx + 1))


def equilibrium(density, speed_x, speed_y, speed_z):
    velocity, weights = lattice()
    comp_x = jnp.asarray(velocity[:, 0], jnp.float32).reshape(27, 1, 1, 1)
    comp_y = jnp.asarray(velocity[:, 1], jnp.float32).reshape(27, 1, 1, 1)
    comp_z = jnp.asarray(velocity[:, 2], jnp.float32).reshape(27, 1, 1, 1)
    factor = jnp.asarray(weights, jnp.float32).reshape(27, 1, 1, 1)
    along = comp_x * speed_x + comp_y * speed_y + comp_z * speed_z
    square = speed_x * speed_x + speed_y * speed_y + speed_z * speed_z
    return factor * density * (1.0 + 3.0 * along + 4.5 * along * along - 1.5 * square)


def collide(pops):
    velocity, weights = lattice()
    first_table = np.concatenate([np.ones((27, 1)), velocity], axis=1)
    moments = jnp.einsum(
        "qm,qzyx->mzyx",
        jnp.asarray(first_table, jnp.float32),
        pops,
        precision=lax.Precision.HIGHEST,
    )
    density = moments[0]
    speed_x = moments[1] / density
    speed_y = moments[2] / density
    speed_z = moments[3] / density
    nonequil = pops - equilibrium(density, speed_x, speed_y, speed_z)
    pair_table = np.stack(
        [
            velocity[:, 0] * velocity[:, 0],
            velocity[:, 1] * velocity[:, 1],
            velocity[:, 2] * velocity[:, 2],
            velocity[:, 0] * velocity[:, 1],
            velocity[:, 0] * velocity[:, 2],
            velocity[:, 1] * velocity[:, 2],
        ],
        axis=1,
    )
    stress = jnp.einsum(
        "qm,qzyx->mzyx",
        jnp.asarray(pair_table, jnp.float32),
        nonequil,
        precision=lax.Precision.HIGHEST,
    )
    strain_sq = (
        stress[0] ** 2
        + stress[1] ** 2
        + stress[2] ** 2
        + 2.0 * (stress[3] ** 2 + stress[4] ** 2 + stress[5] ** 2)
    )
    magnitude = jnp.sqrt(2.0 * strain_sq)
    relax = 0.5 * (
        tau_base
        + jnp.sqrt(
            tau_base * tau_base + 18.0 * root_two * smag_const * smag_const * magnitude / density
        )
    )
    return (pops - nonequil / relax, density)


def shards(pops, solid, profile_table, profile_index):
    velocity, weights = lattice()
    planes, span_cells, stream_cells = solid.shape
    profiles = profile_table.shape[0]
    walls = padded_2(solid, (("gx", 2), ("gy", 1), ("gz", 0)), 1)
    height = lax.axis_index("gz") * planes + jnp.arange(planes, dtype=jnp.int32)[:, None, None]
    depth = planes * lax.axis_size("gz")
    stream_pos = lax.axis_index("gx") * stream_cells + jnp.arange(stream_cells, dtype=jnp.int32)
    sponge = (stream_pos < SPONGE)[None, None, None, :]
    onehot = (profile_index[:, None] == jnp.arange(profiles, dtype=jnp.int32)[None, :]).astype(
        jnp.float32
    )
    target = jnp.einsum("yp,pz->zy", onehot, profile_table, precision=lax.Precision.HIGHEST)[
        :, :, None
    ]
    fluid = (solid == 0)[None]
    rest = jnp.asarray(weights, jnp.float32).reshape(27, 1, 1, 1)
    for step in range(STEPS):
        post, density = collide(pops)
        zeros = jnp.zeros_like(density)
        pinned = equilibrium(density, target + zeros, zeros, zeros)
        post = jnp.where(sponge, pinned, post)
        padded = padded_2(post, (("gx", 3), ("gy", 2), ("gz", 1)), 1)
        pieces = []
        for number in range(27):
            cx, cy, cz = [int(value) for value in velocity[number]]
            source = padded[
                number,
                1 - cz : 1 - cz + planes,
                1 - cy : 1 - cy + span_cells,
                1 - cx : 1 - cx + stream_cells,
            ]
            blocked = (
                walls[
                    1 - cz : 1 - cz + planes,
                    1 - cy : 1 - cy + span_cells,
                    1 - cx : 1 - cx + stream_cells,
                ]
                == 1
            )
            bounce = post[26 - number]
            mirror = padded[
                mirror_of(number),
                1 : 1 + planes,
                1 - cy : 1 - cy + span_cells,
                1 - cx : 1 - cx + stream_cells,
            ]
            value = jnp.where(blocked, bounce, source)
            value = jnp.where(height - cz < 0, bounce, value)
            value = jnp.where(height - cz > depth - 1, mirror, value)
            pieces.append(value)
        pops = jnp.where(fluid, jnp.stack(pieces), rest)
    return pops


def solution(mesh):
    return jax.shard_map(
        shards,
        mesh=mesh,
        in_specs=(P(None, "gz", "gy", "gx"), P("gz", "gy", "gx"), P(None, "gz"), P("gy")),
        out_specs=P(None, "gz", "gy", "gx"),
        check_vma=False,
    )
```

profile of v0, /device:TPU:1, one launch (start us, length us, event | category | flops | bytes accessed | tf_op | source)
XLA Modules:
  0.0 123.9 jit_solution(14279118593568449536)
XLA Ops:
  0.0 0.7 copy-done.5
  0.7 1.6 %fusion.6 = f32[4,4,8,128]{3,0,2,1:T(4,128)S(1)} fusion(f32[27,4,1,1]{0,1,3,2:T(4,128)S(1)} %copy-done.5, f32[27,4,8,128]{3,2,1,0:T(8,128)} %param.25), kind=kOutput, calls=%fused_computation.14 | convolution fusion | flops 5308416 | bytes 508336 | tf_op jit(solution)/shard_map/qm,qzyx->mzyx/dot_general | solution.py:58
  6.0 0.8 fusion.8
  7.0 5.9 %collective-permute-start.1 = (f32[27,4,8,1]{3,2,1,0:T(8,128)S(1)}, f32[27,4,8,1]{3,2,1,0:T(8,128)S(1)}, u32[]{:S(2)}, u32[]{:S(2)}) collective-permute-start(f32[27,4,8,1]{3,2,1,0:T(8,128)S(1)} %get-tuple-element.68), channel_id=1, source_target_pairs={{64,0},{128,64},{192,128},{256,192},{320,256},{384,320},{448,384},... | collective-permute-start | bytes 10376 | tf_op jit(solution)/shard_map/ppermute | solution.py:24
  13.0 1.9 %collective-permute-start = (f32[27,4,8,1]{3,2,1,0:T(8,128)S(1)}, f32[27,4,8,1]{3,2,1,0:T(8,128)S(1)}, u32[]{:S(2)}, u32[]{:S(2)}) collective-permute-start(f32[27,4,8,1]{3,2,1,0:T(8,128)S(1)} %get-tuple-element.67), channel_id=1, source_target_pairs={{0,64},{64,128},{128,192},{192,256},{256,320},{320,384},{384,448},... | collective-permute-start | bytes 10376 | tf_op jit(solution)/shard_map/ppermute | solution.py:23
  15.0 4.6 %collective-permute-start.4 = (s32[4,8,1]{2,1,0:T(8,128)S(1)}, s32[4,8,1]{2,1,0:T(8,128)S(1)}, u32[]{:S(2)}, u32[]{:S(2)}) collective-permute-start(s32[4,8,1]{2,1,0:T(8,128)S(1)} %get-tuple-element.104), channel_id=1, source_target_pairs={{64,0},{128,64},{192,128},{256,192},{320,256},{384,320},{448,384},... | collective-permute-start | bytes 392 | tf_op jit(solution)/shard_map/ppermute | solution.py:24
  19.6 1.9 %collective-permute-start.3 = (s32[4,8,1]{2,1,0:T(8,128)S(1)}, s32[4,8,1]{2,1,0:T(8,128)S(1)}, u32[]{:S(2)}, u32[]{:S(2)}) collective-permute-start(s32[4,8,1]{2,1,0:T(8,128)S(1)} %get-tuple-element.103), channel_id=1, source_target_pairs={{0,64},{64,128},{128,192},{192,256},{256,320},{320,384},{384,448},... | collective-permute-start | bytes 392 | tf_op jit(solution)/shard_map/ppermute | solution.py:23
  21.5 4.2 %collective-permute-done.3 = s32[4,8,1]{2,1,0:T(8,128)S(1)} collective-permute-done((s32[4,8,1]{2,1,0:T(8,128)S(1)}, s32[4,8,1]{2,1,0:T(8,128)S(1)}, u32[]{:S(2)}, u32[]{:S(2)}) %collective-permute-start.3) | collective-permute-done | bytes 160 | tf_op jit(solution)/shard_map/ppermute | solution.py:23
  25.9 13.0 %collective-permute-start.6 = (s32[4,1,130]{2,1,0:T(1,128)S(1)}, s32[4,1,130]{2,1,0:T(1,128)S(1)}, u32[]{:S(2)}, u32[]{:S(2)}) collective-permute-start(s32[4,1,130]{2,1,0:T(1,128)S(1)} %get-tuple-element.94), channel_id=1, source_target_pairs={{4,0},{8,4},{12,8},{16,12},{20,16},{24,20},{28,24},{32,28},{36,32}... | collective-permute-start | bytes 6248 | tf_op jit(solution)/shard_map/ppermute | solution.py:24
  38.8 1.9 %collective-permute-start.5 = (s32[4,1,130]{2,1,0:T(1,128)S(1)}, s32[4,1,130]{2,1,0:T(1,128)S(1)}, u32[]{:S(2)}, u32[]{:S(2)}) collective-permute-start(s32[4,1,130]{2,1,0:T(1,128)S(1)} %get-tuple-element.93), channel_id=1, source_target_pairs={{0,4},{4,8},{8,12},{12,16},{16,20},{20,24},{24,28},{28,32},{32,36}... | collective-permute-start | bytes 6248 | tf_op jit(solution)/shard_map/ppermute | solution.py:23
  40.8 0.8 pad_maximum_fusion.13
  41.6 5.5 %collective-permute-start.2 = (f32[27,4,1,130]{3,2,1,0:T(1,128)S(1)}, f32[27,4,1,130]{3,2,1,0:T(1,128)S(1)}, u32[]{:S(2)}, u32[]{:S(2)}) collective-permute-start(f32[27,4,1,130]{3,2,1,0:T(1,128)S(1)} %get-tuple-element.64), channel_id=1, source_target_pairs={{4,0},{8,4},{12,8},{16,12},{20,16},{24,20},{28,24},{32,28},{36,32}... | collective-permute-start | bytes 168488 | tf_op jit(solution)/shard_map/ppermute | solution.py:24
  47.0 1.9 %collective-permute-start.8 = (f32[27,4,1,130]{3,2,1,0:T(1,128)S(1)}, f32[27,4,1,130]{3,2,1,0:T(1,128)S(1)}, u32[]{:S(2)}, u32[]{:S(2)}) collective-permute-start(f32[27,4,1,130]{3,2,1,0:T(1,128)S(1)} %get-tuple-element.63), channel_id=1, source_target_pairs={{0,4},{4,8},{8,12},{12,16},{16,20},{20,24},{24,28},{28,32},{32,36}... | collective-permute-start | bytes 168488 | tf_op jit(solution)/shard_map/ppermute | solution.py:23
  49.1 6.9 %collective-permute-start.10 = (s32[1,10,130]{2,1,0:T(8,128)S(1)}, s32[1,10,130]{2,1,0:T(8,128)S(1)}, u32[]{:S(2)}, u32[]{:S(2)}) collective-permute-start(s32[1,10,130]{2,1,0:T(8,128)S(1)} %get-tuple-element.91), channel_id=1, source_target_pairs={{0,1},{1,2},{2,3},{3,0},{4,5},{5,6},{6,7},{7,4},{8,9},{9,10},{10,1... | collective-permute-start | bytes 15608 | tf_op jit(solution)/shard_map/ppermute | solution.py:23
  56.0 1.9 %collective-permute-start.7 = (s32[1,10,130]{2,1,0:T(8,128)S(1)}, s32[1,10,130]{2,1,0:T(8,128)S(1)}, u32[]{:S(2)}, u32[]{:S(2)}) collective-permute-start(s32[1,10,130]{2,1,0:T(8,128)S(1)} %get-tuple-element.92), channel_id=1, source_target_pairs={{1,0},{2,1},{3,2},{0,3},{5,4},{6,5},{7,6},{4,7},{9,8},{10,9},{11,1... | collective-permute-start | bytes 15608 | tf_op jit(solution)/shard_map/ppermute | solution.py:24
  58.4 2.8 %collective-permute-start.9 = (f32[27,1,10,130]{3,2,1,0:T(8,128)S(1)}, f32[27,1,10,130]{3,2,1,0:T(8,128)S(1)}, u32[]{:S(2)}, u32[]{:S(2)}) collective-permute-start(f32[27,1,10,130]{3,2,1,0:T(8,128)S(1)} %get-tuple-element.60), channel_id=1, source_target_pairs={{1,0},{2,1},{3,2},{0,3},{5,4},{6,5},{7,6},{4,7},{9,8},{10,9},{11,1... | collective-permute-start | bytes 421208 | tf_op jit(solution)/shard_map/ppermute | solution.py:24
  61.3 1.3 %collective-permute-done.7 = s32[1,10,130]{2,1,0:T(8,128)S(1)} collective-permute-done((s32[1,10,130]{2,1,0:T(8,128)S(1)}, s32[1,10,130]{2,1,0:T(8,128)S(1)}, u32[]{:S(2)}, u32[]{:S(2)}) %collective-permute-start.7) | collective-permute-done | bytes 5232 | tf_op jit(solution)/shard_map/ppermute | solution.py:24
  62.7 2.9 %collective-permute-start.11 = (f32[27,1,10,130]{3,2,1,0:T(8,128)S(1)}, f32[27,1,10,130]{3,2,1,0:T(8,128)S(1)}, u32[]{:S(2)}, u32[]{:S(2)}) collective-permute-start(f32[27,1,10,130]{3,2,1,0:T(8,128)S(1)} %get-tuple-element.59), channel_id=1, source_target_pairs={{0,1},{1,2},{2,3},{3,0},{4,5},{5,6},{6,7},{7,4},{8,9},{9,10},{10,1... | collective-permute-start | bytes 421208 | tf_op jit(solution)/shard_map/ppermute | solution.py:23
  65.7 6.5 %collective-permute-done.9 = f32[27,1,10,130]{3,2,1,0:T(8,128)S(1)} collective-permute-done((f32[27,1,10,130]{3,2,1,0:T(8,128)S(1)}, f32[27,1,10,130]{3,2,1,0:T(8,128)S(1)}, u32[]{:S(2)}, u32[]{:S(2)}) %collective-permute-start.9) | collective-permute-done | bytes 140432 | tf_op jit(solution)/shard_map/ppermute | solution.py:24
  76.8 0.7 fusion.10
  77.6 1.9 %collective-permute-start.13 = (f32[27,4,8,1]{3,2,1,0:T(8,128)S(1)}, f32[27,4,8,1]{3,2,1,0:T(8,128)S(1)}, u32[]{:S(2)}, u32[]{:S(2)}) collective-permute-start(f32[27,4,8,1]{3,2,1,0:T(8,128)S(1)} %get-tuple-element.66), channel_id=1, source_target_pairs={{64,0},{128,64},{192,128},{256,192},{320,256},{384,320},{448,384},... | collective-permute-start | bytes 10376 | tf_op jit(solution)/shard_map/ppermute | solution.py:24
  79.5 3.4 %collective-permute-start.12 = (f32[27,4,8,1]{3,2,1,0:T(8,128)S(1)}, f32[27,4,8,1]{3,2,1,0:T(8,128)S(1)}, u32[]{:S(2)}, u32[]{:S(2)}) collective-permute-start(f32[27,4,8,1]{3,2,1,0:T(8,128)S(1)} %get-tuple-element.65), channel_id=1, source_target_pairs={{0,64},{64,128},{128,192},{192,256},{256,320},{320,384},{384,448},... | collective-permute-start | bytes 10376 | tf_op jit(solution)/shard_map/ppermute | solution.py:23
  82.9 7.3 %collective-permute-done.13 = f32[27,4,8,1]{3,2,1,0:T(8,128)S(1)} collective-permute-done((f32[27,4,8,1]{3,2,1,0:T(8,128)S(1)}, f32[27,4,8,1]{3,2,1,0:T(8,128)S(1)}, u32[]{:S(2)}, u32[]{:S(2)}) %collective-permute-start.13) | collective-permute-done | bytes 3488 | tf_op jit(solution)/shard_map/ppermute | solution.py:24
  90.2 3.0 %collective-permute-done.12 = f32[27,4,8,1]{3,2,1,0:T(8,128)S(1)} collective-permute-done((f32[27,4,8,1]{3,2,1,0:T(8,128)S(1)}, f32[27,4,8,1]{3,2,1,0:T(8,128)S(1)}, u32[]{:S(2)}, u32[]{:S(2)}) %collective-permute-start.12) | collective-permute-done | bytes 3488 | tf_op jit(solution)/shard_map/ppermute | solution.py:23
  93.2 0.7 pad_maximum_fusion.10
  94.0 3.9 %collective-permute-start.14 = (f32[27,4,1,130]{3,2,1,0:T(1,128)S(1)}, f32[27,4,1,130]{3,2,1,0:T(1,128)S(1)}, u32[]{:S(2)}, u32[]{:S(2)}) collective-permute-start(f32[27,4,1,130]{3,2,1,0:T(1,128)S(1)} %get-tuple-element.62), channel_id=1, source_target_pairs={{4,0},{8,4},{12,8},{16,12},{20,16},{24,20},{28,24},{32,28},{36,32}... | collective-permute-start | bytes 168488 | tf_op jit(solution)/shard_map/ppermute | solution.py:24
  97.9 1.9 %collective-permute-start.15 = (f32[27,4,1,130]{3,2,1,0:T(1,128)S(1)}, f32[27,4,1,130]{3,2,1,0:T(1,128)S(1)}, u32[]{:S(2)}, u32[]{:S(2)}) collective-permute-start(f32[27,4,1,130]{3,2,1,0:T(1,128)S(1)} %get-tuple-element.61), channel_id=1, source_target_pairs={{0,4},{4,8},{8,12},{12,16},{16,20},{20,24},{24,28},{28,32},{32,36}... | collective-permute-start | bytes 168488 | tf_op jit(solution)/shard_map/ppermute | solution.py:23
  99.9 5.7 %collective-permute-done.15 = f32[27,4,1,130]{3,2,1,0:T(1,128)S(1)} collective-permute-done((f32[27,4,1,130]{3,2,1,0:T(1,128)S(1)}, f32[27,4,1,130]{3,2,1,0:T(1,128)S(1)}, u32[]{:S(2)}, u32[]{:S(2)}) %collective-permute-start.15) | collective-permute-done | bytes 56192 | tf_op jit(solution)/shard_map/ppermute | solution.py:23
  106.0 5.9 %collective-permute-start.16 = (f32[27,1,10,130]{3,2,1,0:T(8,128)S(1)}, f32[27,1,10,130]{3,2,1,0:T(8,128)S(1)}, u32[]{:S(2)}, u32[]{:S(2)}) collective-permute-start(f32[27,1,10,130]{3,2,1,0:T(8,128)S(1)} %get-tuple-element.58), channel_id=1, source_target_pairs={{1,0},{2,1},{3,2},{0,3},{5,4},{6,5},{7,6},{4,7},{9,8},{10,9},{11,1... | collective-permute-start | bytes 421208 | tf_op jit(solution)/shard_map/ppermute | solution.py:24
  111.9 2.8 %collective-permute-start.17 = (f32[27,1,10,130]{3,2,1,0:T(8,128)S(1)}, f32[27,1,10,130]{3,2,1,0:T(8,128)S(1)}, u32[]{:S(2)}, u32[]{:S(2)}) collective-permute-start(f32[27,1,10,130]{3,2,1,0:T(8,128)S(1)} %get-tuple-element.57), channel_id=1, source_target_pairs={{0,1},{1,2},{2,3},{3,0},{4,5},{5,6},{6,7},{7,4},{8,9},{9,10},{10,1... | collective-permute-start | bytes 421208 | tf_op jit(solution)/shard_map/ppermute | solution.py:23
  114.8 5.5 %collective-permute-done.16 = f32[27,1,10,130]{3,2,1,0:T(8,128)S(1)} collective-permute-done((f32[27,1,10,130]{3,2,1,0:T(8,128)S(1)}, f32[27,1,10,130]{3,2,1,0:T(8,128)S(1)}, u32[]{:S(2)}, u32[]{:S(2)}) %collective-permute-start.16) | collective-permute-done | bytes 140432 | tf_op jit(solution)/shard_map/ppermute | solution.py:24
  123.0 0.9 broadcast_select_fusion
  (116 shorter events, 12.2 us)
Async XLA Ops:
  0.0 4.5 %copy-start = (f32[8,4]{0,1:T(4,128)S(1)}, f32[8,4]{0,1:T(4,128)}, u32[]{:S(2)}) copy-start(f32[8,4]{0,1:T(4,128)} %param.27) | copy-start | bytes 388
  0.0 0.7 copy-start.5
  0.0 2.4 %copy-start.1 = (f32[27,4,8,128]{3,2,1,0:T(8,128)S(1)}, f32[27,4,8,128]{3,2,1,0:T(8,128)}, u32[]{:S(2)}) copy-start(f32[27,4,8,128]{3,2,1,0:T(8,128)} %param.25) | copy-start | bytes 1327108
  2.4 0.7 copy-start.8
  2.4 0.7 copy-start.3
  2.4 0.7 copy-start.6
  2.4 0.7 copy-start.7
  3.1 0.7 copy-start.4
  4.5 0.7 copy-start.11
  5.3 0.7 copy-start.9
  5.4 0.7 copy-start.10
  6.8 8.1 %copy-start.2 = (s32[4,8,128]{2,1,0:T(8,128)S(1)}, s32[4,8,128]{2,1,0:T(8,128)}, u32[]{:S(2)}) copy-start(s32[4,8,128]{2,1,0:T(8,128)} %param.26) | copy-start | bytes 49156
  7.0 33.7 %collective-permute-start.1 = (f32[27,4,8,1]{3,2,1,0:T(8,128)S(1)}, f32[27,4,8,1]{3,2,1,0:T(8,128)S(1)}, u32[]{:S(2)}, u32[]{:S(2)}) collective-permute-start(f32[27,4,8,1]{3,2,1,0:T(8,128)S(1)} %get-tuple-element.68), channel_id=1, source_target_pairs={{64,0},{128,64},{192,128},{256,192},{320,256},{384,320},{448,384},... | collective-permute-start | bytes 10376 | tf_op jit(solution)/shard_map/ppermute | solution.py:24
  13.0 27.8 %collective-permute-start = (f32[27,4,8,1]{3,2,1,0:T(8,128)S(1)}, f32[27,4,8,1]{3,2,1,0:T(8,128)S(1)}, u32[]{:S(2)}, u32[]{:S(2)}) collective-permute-start(f32[27,4,8,1]{3,2,1,0:T(8,128)S(1)} %get-tuple-element.67), channel_id=1, source_target_pairs={{0,64},{64,128},{128,192},{192,256},{256,320},{320,384},{384,448},... | collective-permute-start | bytes 10376 | tf_op jit(solution)/shard_map/ppermute | solution.py:23
  15.0 6.5 %collective-permute-start.4 = (s32[4,8,1]{2,1,0:T(8,128)S(1)}, s32[4,8,1]{2,1,0:T(8,128)S(1)}, u32[]{:S(2)}, u32[]{:S(2)}) collective-permute-start(s32[4,8,1]{2,1,0:T(8,128)S(1)} %get-tuple-element.104), channel_id=1, source_target_pairs={{64,0},{128,64},{192,128},{256,192},{320,256},{384,320},{448,384},... | collective-permute-start | bytes 392 | tf_op jit(solution)/shard_map/ppermute | solution.py:24
  19.6 6.2 %collective-permute-start.3 = (s32[4,8,1]{2,1,0:T(8,128)S(1)}, s32[4,8,1]{2,1,0:T(8,128)S(1)}, u32[]{:S(2)}, u32[]{:S(2)}) collective-permute-start(s32[4,8,1]{2,1,0:T(8,128)S(1)} %get-tuple-element.103), channel_id=1, source_target_pairs={{0,64},{64,128},{128,192},{192,256},{256,320},{320,384},{384,448},... | collective-permute-start | bytes 392 | tf_op jit(solution)/shard_map/ppermute | solution.py:23
  25.9 23.1 %collective-permute-start.6 = (s32[4,1,130]{2,1,0:T(1,128)S(1)}, s32[4,1,130]{2,1,0:T(1,128)S(1)}, u32[]{:S(2)}, u32[]{:S(2)}) collective-permute-start(s32[4,1,130]{2,1,0:T(1,128)S(1)} %get-tuple-element.94), channel_id=1, source_target_pairs={{4,0},{8,4},{12,8},{16,12},{20,16},{24,20},{28,24},{32,28},{36,32}... | collective-permute-start | bytes 6248 | tf_op jit(solution)/shard_map/ppermute | solution.py:24
  38.8 10.1 %collective-permute-start.5 = (s32[4,1,130]{2,1,0:T(1,128)S(1)}, s32[4,1,130]{2,1,0:T(1,128)S(1)}, u32[]{:S(2)}, u32[]{:S(2)}) collective-permute-start(s32[4,1,130]{2,1,0:T(1,128)S(1)} %get-tuple-element.93), channel_id=1, source_target_pairs={{0,4},{4,8},{8,12},{12,16},{16,20},{20,24},{24,28},{28,32},{32,36}... | collective-permute-start | bytes 6248 | tf_op jit(solution)/shard_map/ppermute | solution.py:23
  41.6 16.4 %collective-permute-start.2 = (f32[27,4,1,130]{3,2,1,0:T(1,128)S(1)}, f32[27,4,1,130]{3,2,1,0:T(1,128)S(1)}, u32[]{:S(2)}, u32[]{:S(2)}) collective-permute-start(f32[27,4,1,130]{3,2,1,0:T(1,128)S(1)} %get-tuple-element.64), channel_id=1, source_target_pairs={{4,0},{8,4},{12,8},{16,12},{20,16},{24,20},{28,24},{32,28},{36,32}... | collective-permute-start | bytes 168488 | tf_op jit(solution)/shard_map/ppermute | solution.py:24
  47.0 10.9 %collective-permute-start.8 = (f32[27,4,1,130]{3,2,1,0:T(1,128)S(1)}, f32[27,4,1,130]{3,2,1,0:T(1,128)S(1)}, u32[]{:S(2)}, u32[]{:S(2)}) collective-permute-start(f32[27,4,1,130]{3,2,1,0:T(1,128)S(1)} %get-tuple-element.63), channel_id=1, source_target_pairs={{0,4},{4,8},{8,12},{12,16},{16,20},{20,24},{24,28},{28,32},{32,36}... | collective-permute-start | bytes 168488 | tf_op jit(solution)/shard_map/ppermute | solution.py:23
  49.1 12.2 %collective-permute-start.10 = (s32[1,10,130]{2,1,0:T(8,128)S(1)}, s32[1,10,130]{2,1,0:T(8,128)S(1)}, u32[]{:S(2)}, u32[]{:S(2)}) collective-permute-start(s32[1,10,130]{2,1,0:T(8,128)S(1)} %get-tuple-element.91), channel_id=1, source_target_pairs={{0,1},{1,2},{2,3},{3,0},{4,5},{5,6},{6,7},{7,4},{8,9},{9,10},{10,1... | collective-permute-start | bytes 15608 | tf_op jit(solution)/shard_map/ppermute | solution.py:23
  56.0 6.6 %collective-permute-start.7 = (s32[1,10,130]{2,1,0:T(8,128)S(1)}, s32[1,10,130]{2,1,0:T(8,128)S(1)}, u32[]{:S(2)}, u32[]{:S(2)}) collective-permute-start(s32[1,10,130]{2,1,0:T(8,128)S(1)} %get-tuple-element.92), channel_id=1, source_target_pairs={{1,0},{2,1},{3,2},{0,3},{5,4},{6,5},{7,6},{4,7},{9,8},{10,9},{11,1... | collective-permute-start | bytes 15608 | tf_op jit(solution)/shard_map/ppermute | solution.py:24
  58.4 13.8 %collective-permute-start.9 = (f32[27,1,10,130]{3,2,1,0:T(8,128)S(1)}, f32[27,1,10,130]{3,2,1,0:T(8,128)S(1)}, u32[]{:S(2)}, u32[]{:S(2)}) collective-permute-start(f32[27,1,10,130]{3,2,1,0:T(8,128)S(1)} %get-tuple-element.60), channel_id=1, source_target_pairs={{1,0},{2,1},{3,2},{0,3},{5,4},{6,5},{7,6},{4,7},{9,8},{10,9},{11,1... | collective-permute-start | bytes 421208 | tf_op jit(solution)/shard_map/ppermute | solution.py:24
  62.7 11.3 %collective-permute-start.11 = (f32[27,1,10,130]{3,2,1,0:T(8,128)S(1)}, f32[27,1,10,130]{3,2,1,0:T(8,128)S(1)}, u32[]{:S(2)}, u32[]{:S(2)}) collective-permute-start(f32[27,1,10,130]{3,2,1,0:T(8,128)S(1)} %get-tuple-element.59), channel_id=1, source_target_pairs={{0,1},{1,2},{2,3},{3,0},{4,5},{5,6},{6,7},{7,4},{8,9},{9,10},{10,1... | collective-permute-start | bytes 421208 | tf_op jit(solution)/shard_map/ppermute | solution.py:23
  77.6 12.6 %collective-permute-start.13 = (f32[27,4,8,1]{3,2,1,0:T(8,128)S(1)}, f32[27,4,8,1]{3,2,1,0:T(8,128)S(1)}, u32[]{:S(2)}, u32[]{:S(2)}) collective-permute-start(f32[27,4,8,1]{3,2,1,0:T(8,128)S(1)} %get-tuple-element.66), channel_id=1, source_target_pairs={{64,0},{128,64},{192,128},{256,192},{320,256},{384,320},{448,384},... | collective-permute-start | bytes 10376 | tf_op jit(solution)/shard_map/ppermute | solution.py:24
  79.5 13.7 %collective-permute-start.12 = (f32[27,4,8,1]{3,2,1,0:T(8,128)S(1)}, f32[27,4,8,1]{3,2,1,0:T(8,128)S(1)}, u32[]{:S(2)}, u32[]{:S(2)}) collective-permute-start(f32[27,4,8,1]{3,2,1,0:T(8,128)S(1)} %get-tuple-element.65), channel_id=1, source_target_pairs={{0,64},{64,128},{128,192},{192,256},{256,320},{320,384},{384,448},... | collective-permute-start | bytes 10376 | tf_op jit(solution)/shard_map/ppermute | solution.py:23
  94.0 5.9 %collective-permute-start.14 = (f32[27,4,1,130]{3,2,1,0:T(1,128)S(1)}, f32[27,4,1,130]{3,2,1,0:T(1,128)S(1)}, u32[]{:S(2)}, u32[]{:S(2)}) collective-permute-start(f32[27,4,1,130]{3,2,1,0:T(1,128)S(1)} %get-tuple-element.62), channel_id=1, source_target_pairs={{4,0},{8,4},{12,8},{16,12},{20,16},{24,20},{28,24},{32,28},{36,32}... | collective-permute-start | bytes 168488 | tf_op jit(solution)/shard_map/ppermute | solution.py:24
  97.9 7.6 %collective-permute-start.15 = (f32[27,4,1,130]{3,2,1,0:T(1,128)S(1)}, f32[27,4,1,130]{3,2,1,0:T(1,128)S(1)}, u32[]{:S(2)}, u32[]{:S(2)}) collective-permute-start(f32[27,4,1,130]{3,2,1,0:T(1,128)S(1)} %get-tuple-element.61), channel_id=1, source_target_pairs={{0,4},{4,8},{8,12},{12,16},{16,20},{20,24},{24,28},{28,32},{32,36}... | collective-permute-start | bytes 168488 | tf_op jit(solution)/shard_map/ppermute | solution.py:23
  106.0 14.3 %collective-permute-start.16 = (f32[27,1,10,130]{3,2,1,0:T(8,128)S(1)}, f32[27,1,10,130]{3,2,1,0:T(8,128)S(1)}, u32[]{:S(2)}, u32[]{:S(2)}) collective-permute-start(f32[27,1,10,130]{3,2,1,0:T(8,128)S(1)} %get-tuple-element.58), channel_id=1, source_target_pairs={{1,0},{2,1},{3,2},{0,3},{5,4},{6,5},{7,6},{4,7},{9,8},{10,9},{11,1... | collective-permute-start | bytes 421208 | tf_op jit(solution)/shard_map/ppermute | solution.py:24
  111.9 10.2 %collective-permute-start.17 = (f32[27,1,10,130]{3,2,1,0:T(8,128)S(1)}, f32[27,1,10,130]{3,2,1,0:T(8,128)S(1)}, u32[]{:S(2)}, u32[]{:S(2)}) collective-permute-start(f32[27,1,10,130]{3,2,1,0:T(8,128)S(1)} %get-tuple-element.57), channel_id=1, source_target_pairs={{0,1},{1,2},{2,3},{3,0},{4,5},{5,6},{6,7},{7,4},{8,9},{9,10},{10,1... | collective-permute-start | bytes 421208 | tf_op jit(solution)/shard_map/ppermute | solution.py:23
where the time goes:
time: 125 us; the launch traced here: 124 us
  starting transfers between devices  71.2 us (57%)
  waiting for transfers between devices  33.7 us (27%)
  other arithmetic  10.8 us (9%)
  local copies, waits for them, and re-layouts  3.69 us (3%)
  matrix products  3.57 us (3%)
    ppermute x9, starting transfers between devices, padded_2(): after = lax.ppermute(initial, axis, down)  45.5 us
    ppermute x9, starting transfers between devices, padded_2(): before = lax.ppermute(last, axis, up)  25.7 us
    ppermute x9, waiting for transfers between devices, padded_2(): after = lax.ppermute(initial, axis, down)  20.7 us
    ppermute x9, waiting for transfers between devices, padded_2(): before = lax.ppermute(last, axis, up)  13.1 us
    unnamed x50, other arithmetic  4.77 us
    unnamed x26, local copies, waits for them, and re-layouts  2.99 us
    concatenate x6, other arithmetic, padded_2(): array = jnp.concatenate([before, array, after], axis=dim)  2.56 us
  transfers between devices with their start and end apart: 18, of which 8 were waited for; matrix products, arithmetic and copies ran while one was open for 4% of the time, Pallas kernels for 0%

commit v1 on v0

v1 whole, which is shorter than its diff:
```python
import functools

import jax
import jax.numpy as jnp
from jax import lax
from jax.experimental import pallas as pl
from jax.experimental.pallas import tpu as pltpu
from jax.sharding import PartitionSpec as P

SPONGE = 32
TAU = 0.52
SMAG = 0.17
ROOT_TWO = 1.4142135623730951
WEIGHT = (8.0 / 27.0, 2.0 / 27.0, 1.0 / 54.0, 1.0 / 216.0)
F32 = jnp.float32
SIDES = (-1, 0, 1)
VELOCITY = [(cx, cy, cz) for cz in SIDES for cy in SIDES for cx in SIDES]
DIRS = [(dx, dy, dz) for dx in SIDES for dy in SIDES for dz in SIDES if (dx, dy, dz) != (0, 0, 0)]
Z = 4
Y = 8
X = 128


def num(cx, cy, cz):
    return 9 * (cz + 1) + 3 * (cy + 1) + cx + 1


def weight(q):
    return WEIGHT[sum(c * c for c in VELOCITY[q])]


def lane_of(cy, cz, z):
    return 9 * z + 3 * (cz + 1) + cy + 1


def y_groups():
    table, row = {(1, Z - 1): 0, (-1, 0): 4}, 8
    for z in range(Z):
        for cz in SIDES:
            if (cz, z) not in table:
                table[cz, z] = row
                row += 3
    solid = {Z - 1: 3, 0: 7}
    for z in range(1, Z - 1):
        solid[z] = row
        row += 1
    assert row == 40
    return table, solid


Y_ROW, Y_SOLID = y_groups()


def total(values):
    values = list(values)
    while len(values) > 1:
        values = [a + b for a, b in zip(values[::2], values[1::2])] + (
            [values[-1]] if len(values) % 2 else []
        )
    return values[0]


def collide(f, target, sponge):
    s, d, e = {}, {}, {}
    for cz in SIDES:
        for cy in SIDES:
            lo, mid, hi = (f[num(cx, cy, cz)] for cx in SIDES)
            e[cy, cz] = hi + lo
            s[cy, cz] = e[cy, cz] + mid
            d[cy, cz] = hi - lo
    sy = {cy: total(s[cy, cz] for cz in SIDES) for cy in SIDES}
    sz = {cz: total(s[cy, cz] for cy in SIDES) for cz in SIDES}
    dy = {cy: total(d[cy, cz] for cz in SIDES) for cy in SIDES}
    dz = {cz: total(d[cy, cz] for cy in SIDES) for cz in (-1, 1)}
    rho = sy[-1] + sy[0] + sy[1]
    mx, my, mz = dy[-1] + dy[0] + dy[1], sy[1] - sy[-1], sz[1] - sz[-1]
    inv = 1.0 / rho
    ux, uy, uz = mx * inv, my * inv, mz * inv
    third = rho * (1.0 / 3.0)
    pxx = total(e.values()) - third - mx * ux
    pyy = (sy[1] + sy[-1]) - third - my * uy
    pzz = (sz[1] + sz[-1]) - third - mz * uz
    pxy = dy[1] - dy[-1] - mx * uy
    pxz = dz[1] - dz[-1] - mx * uz
    pyz = (s[1, 1] - s[-1, 1]) - (s[1, -1] - s[-1, -1]) - my * uz
    strain = (pxx * pxx + pyy * pyy + pzz * pzz) + 2.0 * (pxy * pxy + pxz * pxz + pyz * pyz)
    size = jnp.sqrt(2.0 * strain)
    tau = 0.5 * (TAU + jnp.sqrt(TAU * TAU + (18.0 * ROOT_TWO * SMAG * SMAG) * size * inv))
    omega = 1.0 / tau
    keep = 1.0 - omega
    base = 1.0 - 1.5 * (ux * ux + uy * uy + uz * uz)
    gain = omega * rho
    gains = [gain * w for w in WEIGHT]
    wx, wy, wz = 3.0 * ux, 3.0 * uy, 3.0 * uz
    t2 = 1.5 * target * target
    t3 = 3.0 * target
    pin_along = {0: 1.0 - t2, 1: 1.0 + t3 + 2.0 * t2, -1: 1.0 - t3 + 2.0 * t2}
    rhos = [rho * w for w in WEIGHT]
    pins = {}
    for cx in SIDES:
        for rest in range(3):
            pins[cx, rest] = rhos[cx * cx + rest] * pin_along[cx]
    post = [None] * 27
    for q in range(13, 27):
        cx, cy, cz = VELOCITY[q]
        kind = cx * cx + cy * cy + cz * cz
        if q == 13:
            post[q] = f[q] * keep + gains[0] * base
        else:
            along = None
            for c, w in ((cx, wx), (cy, wy), (cz, wz)):
                if c:
                    along = (w if c > 0 else -w) if along is None else (along + w if c > 0 else along - w)
            even = base + 0.5 * along * along
            post[q] = f[q] * keep + gains[kind] * (even + along)
            post[26 - q] = f[26 - q] * keep + gains[kind] * (even - along)
    for q in range(27):
        cx, cy, cz = VELOCITY[q]
        post[q] = jnp.where(sponge, pins[cx, cy * cy + cz * cz], post[q])
    return post


def kernel(
    sizes, pops_hbm, solid_ref, target_ref, out_ref,
    fin, post, xpk, ypk, zr, yr, er, xr, masks,
    in_sem, send_sem, recv_sem,
):
    nx, ny, nz = sizes
    gx, gy, gz = lax.axis_index("gx"), lax.axis_index("gy"), lax.axis_index("gz")
    at_top, at_bottom = gz == nz - 1, gz == 0

    def neighbour(d):
        dx, dy, dz = d
        px = gx if dx == 0 else lax.rem(gx + (dx + nx), nx)
        py = gy if dy == 0 else lax.rem(gy + (dy + ny), ny)
        return px, py, gz + dz

    def along_z(dz, body):
        if dz == 0:
            body()
        else:
            pl.when(jnp.logical_not(at_top if dz > 0 else at_bottom))(body)

    barrier = pltpu.get_barrier_semaphore()
    for dz in SIDES:
        def greet(dz=dz):
            for d in DIRS:
                if d[2] == dz:
                    pl.semaphore_signal(
                        barrier, inc=1, device_id=neighbour(d), device_id_type=pl.DeviceIdType.MESH
                    )
        along_z(dz, greet)

    loads = []
    for z in (0, 3, 1, 2):
        copy = pltpu.make_async_copy(pops_hbm.at[:, z], fin.at[z], in_sem.at[z])
        copy.start()
        loads.append((z, copy))

    row = lax.broadcasted_iota(jnp.int32, (Y, X), 0)
    lane = lax.broadcasted_iota(jnp.int32, (Y, X), 1)
    edge_row = {1: row == 0, -1: row == Y - 1}
    edge_lane = {1: lane == 0, -1: lane == X - 1}
    sponge = (lane < SPONGE - gx * X)
    top_mask = jnp.broadcast_to(at_top, (Y, X)) if False else (row * 0 + gz) == nz - 1
    bottom_mask = (row * 0 + gz) == 0

    def dst_of(step, d):
        dx, dy, dz = d
        if dx:
            return xr.at[step, DIRS.index(d)]
        if dy == 0:
            return zr.at[step, (dz + 1) // 2, pl.ds(0, (10 - step) * Y)]
        if dz == 0:
            return yr.at[step, (dy + 1) // 2]
        return er.at[step, dy + 1 + (dz + 1) // 2]

    def src_of(step, d):
        dx, dy, dz = d
        if dx:
            return xpk.at[step, (dx + 1) // 2]
        if dy == 0:
            if dz > 0:
                return post.at[step, Z - 1, pl.ds(19 * Y, (10 - step) * Y)]
            return post.at[step, 0, pl.ds(step * Y, (10 - step) * Y)]
        if dz == 0:
            return ypk.at[step, (dy + 1) // 2]
        return ypk.at[step, (dy + 1) // 2, pl.ds(0, Y)]

    def message(step, d):
        i = DIRS.index(d)
        return pltpu.make_async_remote_copy(
            src_ref=src_of(step, d), dst_ref=dst_of(step, d),
            send_sem=send_sem.at[step, i], recv_sem=recv_sem.at[step, i],
            device_id=neighbour(d), device_id_type=pl.DeviceIdType.MESH,
        )

    def each(step, chosen, what):
        for dz in SIDES:
            dirs = [d for d in chosen if d[2] == dz]
            if dirs:
                def body(dirs=dirs):
                    for d in dirs:
                        getattr(message(step, d), what)()
                along_z(-dz if what == "wait_recv" else dz, body)

    z_dirs = [d for d in DIRS if d[0] == 0 and d[1] == 0]
    y_dirs = [d for d in DIRS if d[0] == 0 and d[1] != 0]
    x_dirs = [d for d in DIRS if d[0] != 0]

    def put(step, z, values):
        for q in range(27):
            post[step, z, (q + 1) * Y:(q + 2) * Y, :] = values[q]

    def tile(step, z, q):
        return post[step, z, (q + 1) * Y:(q + 2) * Y, :]

    def pack(step, packed, z, values, solid):
        for side in (-1, 1):
            acc = packed[side]
            for cy in SIDES:
                for cz in SIDES:
                    col = lane_of(cy, cz, z)
                    shift = (col - (X - 1 if side > 0 else 0)) % X
                    acc = jnp.where(lane == col, pltpu.roll(values[num(side, cy, cz)], shift, 1), acc)
            if step == 0:
                col = 36 + z
                shift = (col - (X - 1 if side > 0 else 0)) % X
                acc = jnp.where(lane == col, pltpu.roll(solid, shift, 1), acc)
            packed[side] = acc
        for side in (-1, 1):
            own = Y - 1 if side > 0 else 0
            for cz in SIDES:
                start = Y_ROW[cz, z]
                first = (num(-1, side, cz) + 1) * Y + own
                ypk[step, (side + 1) // 2, start:start + 3, :] = post[
                    step, z, pl.ds(first, 3, stride=Y), :
                ]
            if step == 0:
                at = Y_SOLID[z]
                ypk[step, (side + 1) // 2, at:at + 1, :] = post[step, z, own:own + 1, :]

    def exchange(step, plane):
        packed = {side: jnp.zeros((Y, X), F32) for side in (-1, 1)}
        for z in (0, 3, 1, 2):
            values = collide(plane(z), target_ref[z], sponge)
            put(step, z, values)
            solid = None
            if step == 0:
                solid = solid_ref[z].astype(F32)
                post[step, z, 0:Y, :] = solid
                post[step, z, 28 * Y:29 * Y, :] = solid
            pack(step, packed, z, values, solid)
            if z == 3:
                if step == 0:
                    pl.semaphore_wait(barrier, jnp.where(at_top | at_bottom, 17, 26))
                each(step, z_dirs, "start")
        for side in (-1, 1):
            xpk[step, (side + 1) // 2] = packed[side]
        each(step, y_dirs, "start")
        each(step, x_dirs, "start")
        each(step, x_dirs, "wait_recv")
        each(step, y_dirs, "wait_recv")
        each(step, z_dirs, "wait_recv")

    def columns(step):
        result = {}
        for cx in (-1, 1):
            for dz in (0, -1, 1):
                near = xr[step, DIRS.index((cx, 0, dz))]
                for cy in SIDES:
                    got = near
                    if cy:
                        far = xr[step, DIRS.index((cx, cy, dz))]
                        got = pltpu.roll(jnp.where(edge_row[-cy], far, near), cy % Y, 0)
                    if dz == -1:
                        mirrored = pltpu.roll(result[cx, cy, 0], X - 33, 1)
                        got = jnp.where(top_mask, mirrored, got)
                    result[cx, cy, dz] = got
        return result

    def shift(value, cx, cy, line, column, col):
        if cy:
            value = jnp.where(edge_row[cy], line(), pltpu.roll(value, cy % Y, 0))
        if cx:
            spot = 0 if cx > 0 else X - 1
            value = jnp.where(
                edge_lane[cx], pltpu.roll(column, (spot - col) % X, 1), pltpu.roll(value, cx % X, 1)
            )
        return value

    def y_line(step, cy, at):
        return jnp.broadcast_to(yr[step, (cy + 1) // 2, at:at + 1, :], (Y, X))

    def e_line(step, cy, dz, at):
        return jnp.broadcast_to(er[step, cy + 1 + (dz + 1) // 2, at:at + 1, :], (Y, X))

    def build_masks(cols):
        for cx in SIDES:
            for cy in SIDES:
                for z in range(-1, Z + 1):
                    if 0 <= z < Z:
                        dz, col, value = 0, 36 + z, post[0, z, 0:Y, :]
                        line = lambda: y_line(0, cy, Y_SOLID[z])
                    elif z < 0:
                        dz, col, value = 1, 36 + Z - 1, zr[0, 1, 9 * Y:10 * Y, :]
                        line = lambda: e_line(0, cy, 1, 3)
                    else:
                        dz, col, value = -1, 36, zr[0, 0, 0:Y, :]
                        line = lambda: e_line(0, cy, -1, 7)
                    value = shift(value, cx, cy, line, cols.get((cx, cy, dz)), col)
                    if z < 0:
                        value = jnp.where(bottom_mask, 1.0, value)
                    if z == Z:
                        value = jnp.where(top_mask, 0.0, value)
                    masks[(3 * (cy + 1) + cx + 1) * (Z + 2) + z + 1] = value

    def stream(step, z, cols):
        own = post[0, z, 0:Y, :] > 0.5
        result = []
        for q in range(27):
            cx, cy, cz = VELOCITY[q]
            at = z - cz
            if 0 <= at < Z:
                value = tile(step, at, q)
                dz, col = 0, lane_of(cy, cz, at)
                line = lambda: y_line(step, cy, Y_ROW[cz, at] + cx + 1)
            elif at < 0:
                value = zr[step, 1, (q - 18) * Y:(q - 17) * Y, :]
                dz, col = 1, lane_of(cy, cz, Z - 1)
                line = lambda: e_line(step, cy, 1, cx + 1)
            else:
                first = (q + 1 - step) * Y
                value = jnp.where(top_mask, tile(step, Z - 1, num(cx, cy, 1)), zr[step, 0, first:first + Y, :])
                dz, col = -1, lane_of(cy, cz, 0)
                line = lambda: jnp.where(
                    top_mask, y_line(step, cy, Y_ROW[1, Z - 1] + cx + 1), e_line(step, cy, -1, 4 + cx + 1)
                )
            value = shift(value, cx, cy, line, cols.get((cx, cy, dz)), col)
            if q != 13:
                blocked = masks[(3 * (cy + 1) + cx + 1) * (Z + 2) + at + 1] > 0.5
                value = jnp.where(blocked, tile(step, z, 26 - q), value)
            result.append(jnp.where(own, weight(q), value))
        return result

    def first_plane(z):
        dict(loads)[z].wait()
        return [fin[z, q] for q in range(27)]

    exchange(0, first_plane)
    cols = columns(0)
    build_masks(cols)
    exchange(1, lambda z: stream(0, z, cols))
    cols = columns(1)
    for z in range(Z):
        values = stream(1, z, cols)
        for q in range(27):
            out_ref[q, z] = values[q]
    for step in range(2):
        for dirs in (z_dirs, y_dirs, x_dirs):
            each(step, dirs, "wait_send")


def shards(mesh_shape, pops, solid, profile_table, profile_index):
    profiles = profile_table.shape[0]
    onehot = profile_index[:, None] == jnp.arange(profiles, dtype=jnp.int32)[None, :]
    target = jnp.sum(
        jnp.where(onehot[None, :, :], profile_table.T[:, None, :], 0.0), axis=2
    )
    target = jnp.broadcast_to(target[:, :, None], (Z, Y, X))
    vmem = pl.BlockSpec(memory_space=pltpu.VMEM)
    return pl.pallas_call(
        functools.partial(kernel, mesh_shape),
        out_shape=jax.ShapeDtypeStruct(pops.shape, F32),
        in_specs=[pl.BlockSpec(memory_space=pl.ANY), vmem, vmem],
        out_specs=vmem,
        scratch_shapes=[
            pltpu.VMEM((Z, 27, Y, X), F32),
            pltpu.VMEM((2, Z, 29 * Y, X), F32),
            pltpu.VMEM((2, 2, Y, X), F32),
            pltpu.VMEM((2, 2, 40, X), F32),
            pltpu.VMEM((2, 2, 10 * Y, X), F32),
            pltpu.VMEM((2, 2, 40, X), F32),
            pltpu.VMEM((2, 4, Y, X), F32),
            pltpu.VMEM((2, 26, Y, X), F32),
            pltpu.VMEM((9 * (Z + 2), Y, X), F32),
            pltpu.SemaphoreType.DMA((Z,)),
            pltpu.SemaphoreType.DMA((2, 26)),
            pltpu.SemaphoreType.DMA((2, 26)),
        ],
        compiler_params=pltpu.CompilerParams(
            collective_id=0, has_side_effects=True, vmem_limit_bytes=32 * 1024 * 1024
        ),
    )(pops, solid, target)


def solution(mesh):
    sizes = tuple(mesh.shape[axis] for axis in ("gx", "gy", "gz"))
    return jax.shard_map(
        functools.partial(shards, sizes),
        mesh=mesh,
        in_specs=(P(None, "gz", "gy", "gx"), P("gz", "gy", "gx"), P(None, "gz"), P("gy")),
        out_specs=P(None, "gz", "gy", "gx"),
        check_vma=False,
    )
```

time: 125 us -> 31.4 us (0.25)
  starting transfers between devices: 71.2 us -> 0 us
  waiting for transfers between devices: 33.7 us -> 0 us
  Pallas kernels: 0 us -> 28.5 us
  other arithmetic: 10.8 us -> 0.16 us
  matrix products: 3.57 us -> 0 us
    ppermute x18 -> x0, starting transfers between devices: 71.2 us -> none  [the longest x9 45.5 us: padded_2(): after = lax.ppermute(initial, axis, down)]
    ppermute x18 -> x0, waiting for transfers between devices: 33.7 us -> none  [the longest x9 20.7 us: padded_2(): after = lax.ppermute(initial, axis, down)]
    pallas_call x0 -> x1, Pallas kernels: none -> 28.5 us  [shards(): pl.pallas_call(functools.partial(kernel, mesh_shape), out_shape=jax.Shape...]
    unnamed x50 -> x0, other arithmetic: 4.77 us -> none
    dot_general x5 -> x0, matrix products: 3.57 us -> none  [the longest x2 2.2 us: collide(): jnp.einsum('qm,qzyx->mzyx', jnp.asarray(first_table, jnp.float32), pops,...]
    concatenate x6 -> x0, other arithmetic: 2.56 us -> none  [padded_2(): array = jnp.concatenate([before, array, after], axis=dim)]
    select_n x4 -> x0, other arithmetic: 2.42 us -> none  [the longest x2 1.46 us: shards(): post = jnp.where(sponge, pinned, post)]
    unnamed x26 -> x9, local copies, waits for them, and re-layouts: 2.99 us -> 2.44 us
  transfers between devices with their start and end apart: 18 -> 0, of which waited for: 8 -> 0; matrix products, arithmetic and copies ran while one was open for 4% -> 0% of each run, Pallas kernels for 0% -> 0%
where the time goes in v1:
time: 31.4 us; the launch traced here: 31.2 us
  Pallas kernels  28.5 us (91%)
  local copies, waits for them, and re-layouts  2.51 us (8%)
    pallas_call x1, Pallas kernels, shards(): pl.pallas_call(functools.partial(kernel, mesh_shape), out_shape=jax.Shape...  28.5 us
    unnamed x9, local copies, waits for them, and re-layouts  2.44 us

profile of v1, /device:TPU:1, one launch (start us, length us, event | category | flops | bytes accessed | tf_op | source)
XLA Modules:
  0.0 31.2 jit_solution(4075442281987741383)
XLA Ops:
  0.0 0.0 copy-start.3
  0.0 0.0 copy-start.2
  0.0 0.0 copy-start.1
  0.0 0.6 %copy-done.3 = s32[8]{0:T(128)S(1)} copy-done((s32[8]{0:T(128)S(1)}, s32[8]{0:T(128)}, u32[]{:S(2)}) %copy-start.3) | copy-done | bytes 56
  0.7 0.1 iota_compare_fusion
  0.7 0.0 copy-done.2
  0.7 0.1 select_reduce_fusion
  0.8 0.1 broadcast_in_dim.33.target_ref
  0.9 0.0 copy-done.1
  0.9 0.0 copy-start
  0.9 1.0 %copy-done = f32[27,4,8,128]{3,2,1,0:T(8,128)S(1)} copy-done((f32[27,4,8,128]{3,2,1,0:T(8,128)S(1)}, f32[27,4,8,128]{3,2,1,0:T(8,128)}, u32[]{:S(2)}) %copy-start) | copy-done | bytes 442392
  1.9 28.5 %shard_map.46 = f32[27,4,8,128]{3,2,1,0:T(8,128)S(1)} custom-call(f32[27,4,8,128]{3,2,1,0:T(8,128)S(1)} %copy-done, s32[4,8,128]{2,1,0:T(8,128)S(1)} %copy-done.1, f32[4,8,128]{2,1,0:T(8,128)S(1)} %broadcast_in_dim.33.target_ref), custom_call_target="tpu_custom_call" | custom-call | tf_op jit(solution)/shard_map/pallas_call | solution.py:372
  30.4 0.8 %copy.6 = f32[27,4,8,128]{3,2,1,0:T(8,128)} copy(f32[27,4,8,128]{3,2,1,0:T(8,128)S(1)} %shard_map.46) | data formatting | bytes 884736
Async XLA Ops:
  0.0 0.7 %copy-start.3 = (s32[8]{0:T(128)S(1)}, s32[8]{0:T(128)}, u32[]{:S(2)}) copy-start(s32[8]{0:T(128)} %param.7) | copy-start | bytes 100
  0.0 0.7 %copy-start.2 = (f32[8,4]{0,1:T(4,128)S(1)}, f32[8,4]{0,1:T(4,128)}, u32[]{:S(2)}) copy-start(f32[8,4]{0,1:T(4,128)} %param.6) | copy-start | bytes 388
  0.0 0.9 %copy-start.1 = (s32[4,8,128]{2,1,0:T(8,128)S(1)}, s32[4,8,128]{2,1,0:T(8,128)}, u32[]{:S(2)}) copy-start(s32[4,8,128]{2,1,0:T(8,128)} %solid_ref.1) | copy-start | bytes 49156
  0.9 1.0 %copy-start = (f32[27,4,8,128]{3,2,1,0:T(8,128)S(1)}, f32[27,4,8,128]{3,2,1,0:T(8,128)}, u32[]{:S(2)}) copy-start(f32[27,4,8,128]{3,2,1,0:T(8,128)} %pops_hbm.1) | copy-start | bytes 1327108

commit v2 on v1

--- a/solution.py
+++ b/solution.py
@@ -121,8 +121,8 @@
 
 
 def kernel(
-    sizes, pops_hbm, solid_ref, target_ref, out_ref,
-    fin, post, xpk, ypk, zr, yr, er, xr, masks,
+    sizes, pops_hbm, solid_hbm, table_hbm, index_hbm, out_ref,
+    fin, solid_ref, table_ref, index_ref, target_ref, post, xpk, ypk, zr, yr, er, xr, masks,
     in_sem, send_sem, recv_sem,
 ):
     nx, ny, nz = sizes
@@ -151,18 +151,25 @@
                     )
         along_z(dz, greet)
 
-    loads = []
+    small = [
+        pltpu.make_async_copy(src, dst, in_sem.at[Z + i])
+        for i, (src, dst) in enumerate(
+            ((index_hbm, index_ref), (table_hbm, table_ref), (solid_hbm, solid_ref))
+        )
+    ]
+    for copy in small:
+        copy.start()
+    loads = {}
     for z in (0, 3, 1, 2):
-        copy = pltpu.make_async_copy(pops_hbm.at[:, z], fin.at[z], in_sem.at[z])
-        copy.start()
-        loads.append((z, copy))
+        loads[z] = pltpu.make_async_copy(pops_hbm.at[:, z], fin.at[z], in_sem.at[z])
+        loads[z].start()
 
     row = lax.broadcasted_iota(jnp.int32, (Y, X), 0)
     lane = lax.broadcasted_iota(jnp.int32, (Y, X), 1)
     edge_row = {1: row == 0, -1: row == Y - 1}
     edge_lane = {1: lane == 0, -1: lane == X - 1}
     sponge = (lane < SPONGE - gx * X)
-    top_mask = jnp.broadcast_to(at_top, (Y, X)) if False else (row * 0 + gz) == nz - 1
+    top_mask = (row * 0 + gz) == nz - 1
     bottom_mask = (row * 0 + gz) == 0
 
     def dst_of(step, d):
@@ -344,9 +351,20 @@
         return result
 
     def first_plane(z):
-        dict(loads)[z].wait()
+        loads[z].wait()
         return [fin[z, q] for q in range(27)]
 
+    for copy in small:
+        copy.wait()
+    which = row * 0
+    for y in range(Y):
+        which = jnp.where(row == y, index_ref[y], which)
+    for z in range(Z):
+        target = jnp.zeros((Y, X), F32)
+        for p in range(table_ref.shape[1]):
+            entry = jnp.broadcast_to(table_ref[z:z + 1, p:p + 1], (Y, X))
+            target = jnp.where(which == p, entry, target)
+        target_ref[z] = target
     exchange(0, first_plane)
     cols = columns(0)
     build_masks(cols)
@@ -362,20 +380,18 @@
 
 
 def shards(mesh_shape, pops, solid, profile_table, profile_index):
-    profiles = profile_table.shape[0]
-    onehot = profile_index[:, None] == jnp.arange(profiles, dtype=jnp.int32)[None, :]
-    target = jnp.sum(
-        jnp.where(onehot[None, :, :], profile_table.T[:, None, :], 0.0), axis=2
-    )
-    target = jnp.broadcast_to(target[:, :, None], (Z, Y, X))
     vmem = pl.BlockSpec(memory_space=pltpu.VMEM)
     return pl.pallas_call(
         functools.partial(kernel, mesh_shape),
         out_shape=jax.ShapeDtypeStruct(pops.shape, F32),
-        in_specs=[pl.BlockSpec(memory_space=pl.ANY), vmem, vmem],
+        in_specs=[pl.BlockSpec(memory_space=pltpu.HBM)] * 4,
         out_specs=vmem,
         scratch_shapes=[
             pltpu.VMEM((Z, 27, Y, X), F32),
+            pltpu.VMEM((Z, Y, X), jnp.int32),
+            pltpu.VMEM((Z, profile_table.shape[0]), F32),
+            pltpu.SMEM((Y,), jnp.int32),
+            pltpu.VMEM((Z, Y, X), F32),
             pltpu.VMEM((2, Z, 29 * Y, X), F32),
             pltpu.VMEM((2, 2, Y, X), F32),
             pltpu.VMEM((2, 2, 40, X), F32),
@@ -384,14 +400,14 @@
             pltpu.VMEM((2, 4, Y, X), F32),
             pltpu.VMEM((2, 26, Y, X), F32),
             pltpu.VMEM((9 * (Z + 2), Y, X), F32),
-            pltpu.SemaphoreType.DMA((Z,)),
+            pltpu.SemaphoreType.DMA((Z + 3,)),
             pltpu.SemaphoreType.DMA((2, 26)),
             pltpu.SemaphoreType.DMA((2, 26)),
         ],
         compiler_params=pltpu.CompilerParams(
             collective_id=0, has_side_effects=True, vmem_limit_bytes=32 * 1024 * 1024
         ),
-    )(pops, solid, target)
+    )(*[pltpu.with_memory_space_constraint(a, pltpu.HBM) for a in (pops, solid, profile_table.T, profile_index)])
 
 
 def solution(mesh):

time: 31.4 us -> 29.4 us (0.936)
  local copies, waits for them, and re-layouts: 2.51 us -> 0.76 us
    unnamed x9 -> x1, local copies, waits for them, and re-layouts: 2.44 us -> 0.76 us
where the time goes in v2:
time: 29.4 us; the launch traced here: 29.3 us
  Pallas kernels  28.5 us (97%)
  local copies, waits for them, and re-layouts  0.76 us (3%)
    pallas_call x1, Pallas kernels, shards(): pl.pallas_call(functools.partial(kernel, mesh_shape), out_shape=jax.Shape...  28.5 us
    unnamed x1, local copies, waits for them, and re-layouts  0.76 us

profile of v2, /device:TPU:1, one launch (start us, length us, event | category | flops | bytes accessed | tf_op | source)
XLA Modules:
  0.0 29.3 jit_solution(3409387804309164415)
XLA Ops:
  0.0 28.5 %shard_map.46 = f32[27,4,8,128]{3,2,1,0:T(8,128)S(1)} custom-call(f32[27,4,8,128]{3,2,1,0:T(8,128)} %pops_hbm.1, s32[4,8,128]{2,1,0:T(8,128)} %solid_hbm.1, f32[4,8]{1,0:T(4,128)} %bitcast.1, s32[8]{0:T(128)} %index_hbm.1), custom_call_target="tpu_custom_call" | custom-call | tf_op jit(solution)/shard_map/pallas_call | solution.py:384
  28.5 0.8 %copy.6 = f32[27,4,8,128]{3,2,1,0:T(8,128)} copy(f32[27,4,8,128]{3,2,1,0:T(8,128)S(1)} %shard_map.46) | data formatting | bytes 884736

commit v3 on v2

--- a/solution.py
+++ b/solution.py
@@ -16,6 +16,7 @@
 SIDES = (-1, 0, 1)
 VELOCITY = [(cx, cy, cz) for cz in SIDES for cy in SIDES for cx in SIDES]
 DIRS = [(dx, dy, dz) for dx in SIDES for dy in SIDES for dz in SIDES if (dx, dy, dz) != (0, 0, 0)]
+FAR_FIRST = sorted(DIRS, key=lambda d: (d[0] == 0, d[1] == 0, d[2] == 0))
 Z = 4
 Y = 8
 X = 128
@@ -142,9 +143,9 @@
             pl.when(jnp.logical_not(at_top if dz > 0 else at_bottom))(body)
 
     barrier = pltpu.get_barrier_semaphore()
-    for dz in SIDES:
+    for dz in (0, -1, 1):
         def greet(dz=dz):
-            for d in DIRS:
+            for d in FAR_FIRST:
                 if d[2] == dz:
                     pl.semaphore_signal(
                         barrier, inc=1, device_id=neighbour(d), device_id_type=pl.DeviceIdType.MESH
@@ -172,27 +173,30 @@
     top_mask = (row * 0 + gz) == nz - 1
     bottom_mask = (row * 0 + gz) == 0
 
+    def rows_to(dy):
+        return pl.ds(0, Y) if dy == 0 else pl.ds(Y - 1 if dy > 0 else 0, 1)
+
     def dst_of(step, d):
         dx, dy, dz = d
         if dx:
-            return xr.at[step, DIRS.index(d)]
+            return xr.at[step, DIRS.index(d), rows_to(dy)]
         if dy == 0:
             return zr.at[step, (dz + 1) // 2, pl.ds(0, (10 - step) * Y)]
         if dz == 0:
-            return yr.at[step, (dy + 1) // 2]
-        return er.at[step, dy + 1 + (dz + 1) // 2]
+            return yr.at[step, (dy + 1) // 2, pl.ds(0, 40 - 2 * step)]
+        return er.at[step, dy + 1 + (dz + 1) // 2, pl.ds(0 if dz > 0 else 4, 4 - step)]
 
     def src_of(step, d):
         dx, dy, dz = d
         if dx:
-            return xpk.at[step, (dx + 1) // 2]
+            return xpk.at[step, (dx + 1) // 2, rows_to(dy)]
         if dy == 0:
             if dz > 0:
                 return post.at[step, Z - 1, pl.ds(19 * Y, (10 - step) * Y)]
             return post.at[step, 0, pl.ds(step * Y, (10 - step) * Y)]
         if dz == 0:
-            return ypk.at[step, (dy + 1) // 2]
-        return ypk.at[step, (dy + 1) // 2, pl.ds(0, Y)]
+            return ypk.at[step, (dy + 1) // 2, pl.ds(0, 40 - 2 * step)]
+        return ypk.at[step, (dy + 1) // 2, pl.ds(0 if dz > 0 else 4, 4 - step)]
 
     def message(step, d):
         i = DIRS.index(d)
@@ -203,8 +207,8 @@
         )
 
     def each(step, chosen, what):
-        for dz in SIDES:
-            dirs = [d for d in chosen if d[2] == dz]
+        for dz in (0, -1, 1):
+            dirs = [d for d in FAR_FIRST if d in chosen and d[2] == dz]
             if dirs:
                 def body(dirs=dirs):
                     for d in dirs:
@@ -258,14 +262,16 @@
                 post[step, z, 0:Y, :] = solid
                 post[step, z, 28 * Y:29 * Y, :] = solid
             pack(step, packed, z, values, solid)
-            if z == 3:
-                if step == 0:
-                    pl.semaphore_wait(barrier, jnp.where(at_top | at_bottom, 17, 26))
+            if z == 3 and step == 1:
                 each(step, z_dirs, "start")
         for side in (-1, 1):
             xpk[step, (side + 1) // 2] = packed[side]
+        if step == 0:
+            pl.semaphore_wait(barrier, jnp.where(at_top | at_bottom, 17, 26))
+        each(step, x_dirs, "start")
+        if step == 0:
+            each(step, z_dirs, "start")
         each(step, y_dirs, "start")
-        each(step, x_dirs, "start")
         each(step, x_dirs, "wait_recv")
         each(step, y_dirs, "wait_recv")
         each(step, z_dirs, "wait_recv")

time: 29.4 us -> 28.8 us (0.980)
  Pallas kernels: 28.5 us -> 27.8 us
    pallas_call x1, Pallas kernels: 28.5 us -> 27.8 us  [shards(): pl.pallas_call(functools.partial(kernel, mesh_shape), out_shape=jax.Shape...]
where the time goes in v3:
time: 28.8 us; the launch traced here: 28.6 us
  Pallas kernels  27.8 us (97%)
  local copies, waits for them, and re-layouts  0.76 us (3%)
    pallas_call x1, Pallas kernels, shards(): pl.pallas_call(functools.partial(kernel, mesh_shape), out_shape=jax.Shape...  27.8 us
    unnamed x1, local copies, waits for them, and re-layouts  0.76 us

profile of v3, /device:TPU:1, one launch (start us, length us, event | category | flops | bytes accessed | tf_op | source)
XLA Modules:
  0.0 28.6 jit_solution(5889558593478216896)
XLA Ops:
  0.0 27.8 %shard_map.46 = f32[27,4,8,128]{3,2,1,0:T(8,128)S(1)} custom-call(f32[27,4,8,128]{3,2,1,0:T(8,128)} %pops_hbm.1, s32[4,8,128]{2,1,0:T(8,128)} %solid_hbm.1, f32[4,8]{1,0:T(4,128)} %bitcast.1, s32[8]{0:T(128)} %index_hbm.1), custom_call_target="tpu_custom_call" | custom-call | tf_op jit(solution)/shard_map/pallas_call | solution.py:390
  27.9 0.8 %copy.6 = f32[27,4,8,128]{3,2,1,0:T(8,128)} copy(f32[27,4,8,128]{3,2,1,0:T(8,128)S(1)} %shard_map.46) | data formatting | bytes 884736

commit v4 on v3

--- a/solution.py
+++ b/solution.py
@@ -121,12 +121,131 @@
     return post
 
 
+def streaming(step, pre, post, zr, yr, er, xr, masks, own_ref, at_top, at_bottom):
+    row = lax.broadcasted_iota(jnp.int32, (Y, X), 0)
+    lane = lax.broadcasted_iota(jnp.int32, (Y, X), 1)
+    edge_row = {1: row == 0, -1: row == Y - 1}
+    edge_lane = {1: lane == 0, -1: lane == X - 1}
+    top_mask = (row * 0 + at_top.astype(jnp.int32)) == 1
+    bottom_mask = (row * 0 + at_bottom.astype(jnp.int32)) == 1
+
+    def tile(z, q):
+        return post[z, (q + 1) * Y:(q + 2) * Y, :]
+
+    def columns():
+        result = {}
+        for cx in (-1, 1):
+            for dz in (0, -1, 1):
+                near = xr[DIRS.index((cx, 0, dz))]
+                for cy in SIDES:
+                    got = near
+                    if cy:
+                        far = xr[DIRS.index((cx, cy, dz))]
+                        got = pltpu.roll(jnp.where(edge_row[-cy], far, near), cy % Y, 0)
+                    if dz == -1:
+                        mirrored = pltpu.roll(result[cx, cy, 0], X - 33, 1)
+                        got = jnp.where(top_mask, mirrored, got)
+                    result[cx, cy, dz] = got
+        return result
+
+    def moved(value, cx, cy, line):
+        if cy:
+            value = jnp.where(edge_row[cy], line(), pltpu.roll(value, cy % Y, 0))
+        return pltpu.roll(value, cx % X, 1) if cx else value
+
+    def joined(value, cx, column, col):
+        spot = 0 if cx > 0 else X - 1
+        return jnp.where(edge_lane[cx], pltpu.roll(column, (spot - col) % X, 1), value)
+
+    def y_line(cy, at):
+        return jnp.broadcast_to(yr[(cy + 1) // 2, at:at + 1, :], (Y, X))
+
+    def e_line(cy, dz, at):
+        return jnp.broadcast_to(er[cy + 1 + (dz + 1) // 2, at:at + 1, :], (Y, X))
+
+    def closed(value, z):
+        if z < 0:
+            return jnp.where(bottom_mask, 1.0, value)
+        return jnp.where(top_mask, 0.0, value) if z == Z else value
+
+    def mask_at(cx, cy, z):
+        return (3 * (cy + 1) + cx + 1) * (Z + 2) + z + 1
+
+    def early_masks():
+        for cy in SIDES:
+            for z in range(-1, Z + 1):
+                if 0 <= z < Z:
+                    value = own_ref[z]
+                    line = lambda: y_line(cy, Y_SOLID[z])
+                elif z < 0:
+                    value = zr[1, 9 * Y:10 * Y, :]
+                    line = lambda: e_line(cy, 1, 3)
+                else:
+                    value = zr[0, 0:Y, :]
+                    line = lambda: e_line(cy, -1, 7)
+                value = moved(value, 0, cy, line)
+                for cx in SIDES:
+                    got = moved(value, cx, 0, None)
+                    masks[mask_at(cx, cy, z)] = got if cx else closed(got, z)
+
+    def late_masks(cols):
+        for cx in (-1, 1):
+            for cy in SIDES:
+                for z in range(-1, Z + 1):
+                    dz, col = (0, 36 + z) if 0 <= z < Z else (1, 36 + Z - 1) if z < 0 else (-1, 36)
+                    at = mask_at(cx, cy, z)
+                    masks[at] = closed(joined(masks[at], cx, cols[cx, cy, dz], col), z)
+
+    def settled(value, z, q):
+        cx, cy, cz = VELOCITY[q]
+        if q != 13:
+            blocked = masks[mask_at(cx, cy, z - cz)] > 0.5
+            value = jnp.where(blocked, tile(z, 26 - q), value)
+        return jnp.where(own_ref[z] > 0.5, weight(q), value)
+
+    def early(z):
+        for q in range(27):
+            cx, cy, cz = VELOCITY[q]
+            at = z - cz
+            if 0 <= at < Z:
+                value = tile(at, q)
+                line = lambda: y_line(cy, Y_ROW[cz, at] + cx + 1)
+            elif at < 0:
+                value = zr[1, (q - 18) * Y:(q - 17) * Y, :]
+                line = lambda: e_line(cy, 1, cx + 1)
+            else:
+                first = (q + 1 - step) * Y
+                value = jnp.where(top_mask, tile(Z - 1, num(cx, cy, 1)), zr[0, first:first + Y, :])
+                line = lambda: jnp.where(
+                    top_mask, y_line(cy, Y_ROW[1, Z - 1] + cx + 1), e_line(cy, -1, 4 + cx + 1)
+                )
+            value = moved(value, cx, cy, line)
+            pre[z, q] = value if cx else settled(value, z, q)
+
+    def late(z, cols):
+        result = []
+        for q in range(27):
+            cx, cy, cz = VELOCITY[q]
+            value = pre[z, q]
+            if cx:
+                at = z - cz
+                dz, source = (0, at) if 0 <= at < Z else (1, Z - 1) if at < 0 else (-1, 0)
+                value = joined(value, cx, cols[cx, cy, dz], lane_of(cy, cz, source))
+                value = settled(value, z, q)
+            result.append(value)
+        return result
+
+    return columns, early_masks, late_masks, early, late
+
+
 def kernel(
-    sizes, pops_hbm, solid_hbm, table_hbm, index_hbm, out_ref,
-    fin, solid_ref, table_ref, index_ref, target_ref, post, xpk, ypk, zr, yr, er, xr, masks,
+    sizes, pops_hbm, solid_hbm, table_hbm, index_hbm,
+    pre1, post1, zr1, yr1, er1, xr1, masks, own_ref,
+    fin, solid_ref, table_ref, index_ref, target_ref, pre0, post0, zr0, yr0, er0, xr0, xpk, ypk,
     in_sem, send_sem, recv_sem,
 ):
     nx, ny, nz = sizes
+    post, zr, yr, er, xr = (post0, post1), (zr0, zr1), (yr0, yr1), (er0, er1), (xr0, xr1)
     gx, gy, gz = lax.axis_index("gx"), lax.axis_index("gy"), lax.axis_index("gz")
     at_top, at_bottom = gz == nz - 1, gz == 0
 
@@ -167,11 +286,7 @@
 
     row = lax.broadcasted_iota(jnp.int32, (Y, X), 0)
     lane = lax.broadcasted_iota(jnp.int32, (Y, X), 1)
-    edge_row = {1: row == 0, -1: row == Y - 1}
-    edge_lane = {1: lane == 0, -1: lane == X - 1}
     sponge = (lane < SPONGE - gx * X)
-    top_mask = (row * 0 + gz) == nz - 1
-    bottom_mask = (row * 0 + gz) == 0
 
     def rows_to(dy):
         return pl.ds(0, Y) if dy == 0 else pl.ds(Y - 1 if dy > 0 else 0, 1)
@@ -179,12 +294,12 @@
     def dst_of(step, d):
         dx, dy, dz = d
         if dx:
-            return xr.at[step, DIRS.index(d), rows_to(dy)]
+            return xr[step].at[DIRS.index(d), rows_to(dy)]
         if dy == 0:
-            return zr.at[step, (dz + 1) // 2, pl.ds(0, (10 - step) * Y)]
+            return zr[step].at[(dz + 1) // 2, pl.ds(0, (10 - step) * Y)]
         if dz == 0:
-            return yr.at[step, (dy + 1) // 2, pl.ds(0, 40 - 2 * step)]
-        return er.at[step, dy + 1 + (dz + 1) // 2, pl.ds(0 if dz > 0 else 4, 4 - step)]
+            return yr[step].at[(dy + 1) // 2, pl.ds(0, 40 - 2 * step)]
+        return er[step].at[dy + 1 + (dz + 1) // 2, pl.ds(0 if dz > 0 else 4, 4 - step)]
 
     def src_of(step, d):
         dx, dy, dz = d
@@ -192,8 +307,8 @@
             return xpk.at[step, (dx + 1) // 2, rows_to(dy)]
         if dy == 0:
             if dz > 0:
-                return post.at[step, Z - 1, pl.ds(19 * Y, (10 - step) * Y)]
-            return post.at[step, 0, pl.ds(step * Y, (10 - step) * Y)]
+                return post[step].at[Z - 1, pl.ds(19 * Y, (10 - step) * Y)]
+            return post[step].at[0, pl.ds(step * Y, (10 - step) * Y)]
         if dz == 0:
             return ypk.at[step, (dy + 1) // 2, pl.ds(0, 40 - 2 * step)]
         return ypk.at[step, (dy + 1) // 2, pl.ds(0 if dz > 0 else 4, 4 - step)]
@@ -221,10 +336,7 @@
 
     def put(step, z, values):
         for q in range(27):
-            post[step, z, (q + 1) * Y:(q + 2) * Y, :] = values[q]
-
-    def tile(step, z, q):
-        return post[step, z, (q + 1) * Y:(q + 2) * Y, :]
+            post[step][z, (q + 1) * Y:(q + 2) * Y, :] = values[q]
 
     def pack(step, packed, z, values, solid):
         for side in (-1, 1):
@@ -244,12 +356,12 @@
             for cz in SIDES:
                 start = Y_ROW[cz, z]
                 first = (num(-1, side, cz) + 1) * Y + own
-                ypk[step, (side + 1) // 2, start:start + 3, :] = post[
-                    step, z, pl.ds(first, 3, stride=Y), :
+                ypk[step, (side + 1) // 2, start:start + 3, :] = post[step][
+                    z, pl.ds(first, 3, stride=Y), :
                 ]
             if step == 0:
                 at = Y_SOLID[z]
-                ypk[step, (side + 1) // 2, at:at + 1, :] = post[step, z, own:own + 1, :]
+                ypk[step, (side + 1) // 2, at:at + 1, :] = post[step][z, own:own + 1, :]
 
     def exchange(step, plane):
         packed = {side: jnp.zeros((Y, X), F32) for side in (-1, 1)}
@@ -259,8 +371,9 @@
             solid = None
             if step == 0:
                 solid = solid_ref[z].astype(F32)
-                post[step, z, 0:Y, :] = solid
-                post[step, z, 28 * Y:29 * Y, :] = solid
+                post[step][z, 0:Y, :] = solid
+                own_ref[z] = solid
+                post[step][z, 28 * Y:29 * Y, :] = solid
             pack(step, packed, z, values, solid)
             if z == 3 and step == 1:
                 each(step, z_dirs, "start")
@@ -272,89 +385,13 @@
         if step == 0:
             each(step, z_dirs, "start")
         each(step, y_dirs, "start")
-        each(step, x_dirs, "wait_recv")
         each(step, y_dirs, "wait_recv")
         each(step, z_dirs, "wait_recv")
-
-    def columns(step):
-        result = {}
-        for cx in (-1, 1):
-            for dz in (0, -1, 1):
-                near = xr[step, DIRS.index((cx, 0, dz))]
-                for cy in SIDES:
-                    got = near
-                    if cy:
-                        far = xr[step, DIRS.index((cx, cy, dz))]
-                        got = pltpu.roll(jnp.where(edge_row[-cy], far, near), cy % Y, 0)
-                    if dz == -1:
-                        mirrored = pltpu.roll(result[cx, cy, 0], X - 33, 1)
-                        got = jnp.where(top_mask, mirrored, got)
-                    result[cx, cy, dz] = got
-        return result
-
-    def shift(value, cx, cy, line, column, col):
-        if cy:
-            value = jnp.where(edge_row[cy], line(), pltpu.roll(value, cy % Y, 0))
-        if cx:
-            spot = 0 if cx > 0 else X - 1
-            value = jnp.where(
-                edge_lane[cx], pltpu.roll(column, (spot - col) % X, 1), pltpu.roll(value, cx % X, 1)
-            )
-        return value
-
-    def y_line(step, cy, at):
-        return jnp.broadcast_to(yr[step, (cy + 1) // 2, at:at + 1, :], (Y, X))
-
-    def e_line(step, cy, dz, at):
-        return jnp.broadcast_to(er[step, cy + 1 + (dz + 1) // 2, at:at + 1, :], (Y, X))
-
-    def build_masks(cols):
-        for cx in SIDES:
-            for cy in SIDES:
-                for z in range(-1, Z + 1):
-                    if 0 <= z < Z:
-                        dz, col, value = 0, 36 + z, post[0, z, 0:Y, :]
-                        line = lambda: y_line(0, cy, Y_SOLID[z])
-                    elif z < 0:
-                        dz, col, value = 1, 36 + Z - 1, zr[0, 1, 9 * Y:10 * Y, :]
-                        line = lambda: e_line(0, cy, 1, 3)
-                    else:
-                        dz, col, value = -1, 36, zr[0, 0, 0:Y, :]
-                        line = lambda: e_line(0, cy, -1, 7)
-                    value = shift(value, cx, cy, line, cols.get((cx, cy, dz)), col)
-                    if z < 0:
-                        value = jnp.where(bottom_mask, 1.0, value)
-                    if z == Z:
-                        value = jnp.where(top_mask, 0.0, value)
-                    masks[(3 * (cy + 1) + cx + 1) * (Z + 2) + z + 1] = value
-
-    def stream(step, z, cols):
-        own = post[0, z, 0:Y, :] > 0.5
-        result = []
-        for q in range(27):
-            cx, cy, cz = VELOCITY[q]
-            at = z - cz
-            if 0 <= at < Z:
-                value = tile(step, at, q)
-                dz, col = 0, lane_of(cy, cz, at)
-                line = lambda: y_line(step, cy, Y_ROW[cz, at] + cx + 1)
-            elif at < 0:
-                value = zr[step, 1, (q - 18) * Y:(q - 17) * Y, :]
-                dz, col = 1, lane_of(cy, cz, Z - 1)
-                line = lambda: e_line(step, cy, 1, cx + 1)
-            else:
-                first = (q + 1 - step) * Y
-                value = jnp.where(top_mask, tile(step, Z - 1, num(cx, cy, 1)), zr[step, 0, first:first + Y, :])
-                dz, col = -1, lane_of(cy, cz, 0)
-                line = lambda: jnp.where(
-                    top_mask, y_line(step, cy, Y_ROW[1, Z - 1] + cx + 1), e_line(step, cy, -1, 4 + cx + 1)
-                )
-            value = shift(value, cx, cy, line, cols.get((cx, cy, dz)), col)
-            if q != 13:
-                blocked = masks[(3 * (cy + 1) + cx + 1) * (Z + 2) + at + 1] > 0.5
-                value = jnp.where(blocked, tile(step, z, 26 - q), value)
-            result.append(jnp.where(own, weight(q), value))
-        return result
+        if step == 0:
+            early_masks[0]()
+        for z in range(Z):
+            early[step](z)
+        each(step, x_dirs, "wait_recv")
 
     def first_plane(z):
         loads[z].wait()
@@ -371,41 +408,57 @@
             entry = jnp.broadcast_to(table_ref[z:z + 1, p:p + 1], (Y, X))
             target = jnp.where(which == p, entry, target)
         target_ref[z] = target
+    columns, early_masks, late_masks, early, late = zip(*(
+        streaming(
+            step, (pre0, pre1)[step], post[step], zr[step], yr[step], er[step], xr[step],
+            masks, own_ref, at_top, at_bottom,
+        )
+        for step in range(2)
+    ))
     exchange(0, first_plane)
-    cols = columns(0)
-    build_masks(cols)
-    exchange(1, lambda z: stream(0, z, cols))
-    cols = columns(1)
-    for z in range(Z):
-        values = stream(1, z, cols)
-        for q in range(27):
-            out_ref[q, z] = values[q]
+    cols = columns[0]()
+    late_masks[0](cols)
+    exchange(1, lambda z: late[0](z, cols))
     for step in range(2):
         for dirs in (z_dirs, y_dirs, x_dirs):
             each(step, dirs, "wait_send")
 
 
+def last(nz, pre, post, zr, yr, er, xr, masks, own_ref, out_hbm, buf, sem):
+    gz = lax.axis_index("gz")
+    columns, _, _, _, late = streaming(
+        1, pre, post, zr, yr, er, xr, masks, own_ref, gz == nz - 1, gz == 0
+    )
+    cols = columns()
+    copies = []
+    for z in range(Z):
+        values = late(z, cols)
+        for q in range(27):
+            buf[z, q] = values[q]
+        copies.append(pltpu.make_async_copy(buf.at[z], out_hbm.at[:, z], sem.at[z]))
+        copies[-1].start()
+    for copy in copies:
+        copy.wait()
+
+
 def shards(mesh_shape, pops, solid, profile_table, profile_index):
     vmem = pl.BlockSpec(memory_space=pltpu.VMEM)
-    return pl.pallas_call(
+    step_shapes = [(Z, 27, Y, X), (Z, 29 * Y, X), (2, 10 * Y, X), (2, 40, X), (4, Y, X), (26, Y, X)]
+    kept_shapes = step_shapes + [(9 * (Z + 2), Y, X), (Z, Y, X)]
+    kept = pl.pallas_call(
         functools.partial(kernel, mesh_shape),
-        out_shape=jax.ShapeDtypeStruct(pops.shape, F32),
+        out_shape=[jax.ShapeDtypeStruct(shape, F32) for shape in kept_shapes],
         in_specs=[pl.BlockSpec(memory_space=pltpu.HBM)] * 4,
-        out_specs=vmem,
+        out_specs=[vmem] * len(kept_shapes),
         scratch_shapes=[
             pltpu.VMEM((Z, 27, Y, X), F32),
             pltpu.VMEM((Z, Y, X), jnp.int32),
             pltpu.VMEM((Z, profile_table.shape[0]), F32),
             pltpu.SMEM((Y,), jnp.int32),
             pltpu.VMEM((Z, Y, X), F32),
-            pltpu.VMEM((2, Z, 29 * Y, X), F32),
+            *[pltpu.VMEM(shape, F32) for shape in step_shapes],
             pltpu.VMEM((2, 2, Y, X), F32),
             pltpu.VMEM((2, 2, 40, X), F32),
-            pltpu.VMEM((2, 2, 10 * Y, X), F32),
-            pltpu.VMEM((2, 2, 40, X), F32),
-            pltpu.VMEM((2, 4, Y, X), F32),
-            pltpu.VMEM((2, 26, Y, X), F32),
-            pltpu.VMEM((9 * (Z + 2), Y, X), F32),
             pltpu.SemaphoreType.DMA((Z + 3,)),
             pltpu.SemaphoreType.DMA((2, 26)),
             pltpu.SemaphoreType.DMA((2, 26)),
@@ -413,7 +466,18 @@
         compiler_params=pltpu.CompilerParams(
             collective_id=0, has_side_effects=True, vmem_limit_bytes=32 * 1024 * 1024
         ),
-    )(*[pltpu.with_memory_space_constraint(a, pltpu.HBM) for a in (pops, solid, profile_table.T, profile_index)])
+    )(*[
+        pltpu.with_memory_space_constraint(a, pltpu.HBM)
+        for a in (pops, solid, profile_table.T, profile_index)
+    ])
+    return pl.pallas_call(
+        functools.partial(last, mesh_shape[2]),
+        out_shape=jax.ShapeDtypeStruct(pops.shape, F32),
+        in_specs=[vmem] * len(kept_shapes),
+        out_specs=pl.BlockSpec(memory_space=pl.ANY),
+        scratch_shapes=[pltpu.VMEM((Z, 27, Y, X), F32), pltpu.SemaphoreType.DMA((Z,))],
+        compiler_params=pltpu.CompilerParams(vmem_limit_bytes=32 * 1024 * 1024),
+    )(*kept)
 
 
 def solution(mesh):

time: 28.8 us -> 28.4 us (0.986)
  local copies, waits for them, and re-layouts: 0.76 us -> 0 us
  Pallas kernels: 27.8 us -> 28.3 us
    unnamed x1 -> x0, local copies, waits for them, and re-layouts: 0.76 us -> none
    pallas_call x1 -> x2, Pallas kernels: 27.8 us -> 28.3 us  [the longest x1 27.4 us: shards(): pl.pallas_call(functools.partial(kernel, mesh_shape), out_shape=[jax.Shap...]
where the time goes in v4:
time: 28.4 us; the launch traced here: 28.3 us
  Pallas kernels  28.3 us (100%)
    pallas_call x1, Pallas kernels, shards(): pl.pallas_call(functools.partial(kernel, mesh_shape), out_shape=[jax.Shap...  27.4 us
    pallas_call x1, Pallas kernels, shards(): pl.pallas_call(functools.partial(last, mesh_shape[2]), out_shape=jax.Shap...  0.89 us

profile of v4, /device:TPU:1, one launch (start us, length us, event | category | flops | bytes accessed | tf_op | source)
XLA Modules:
  0.0 28.3 jit_solution(5207434148092462229)
XLA Ops:
  0.0 27.4 %shard_map.46 = (f32[4,27,8,128]{3,2,1,0:T(8,128)S(1)}, f32[4,232,128]{2,1,0:T(8,128)S(1)}, f32[2,80,128]{2,1,0:T(8,128)S(1)}, f32[2,40,128]{2,1,0:T(8,128)S(1)}...) custom-call(f32[27,4,8,128]{3,2,1,0:T(8,128)} %pops_hbm.1, ...), custom_call_target="tpu_custom_call" | custom-call | tf_op jit(solution)/shard_map/pallas_call | solution.py:448
  27.4 0.9 %shard_map.47 = f32[27,4,8,128]{3,2,1,0:T(8,128)} custom-call(f32[4,27,8,128]{3,2,1,0:T(8,128)S(1)} %get-tuple-element.13.pre, f32[4,232,128]{2,1,0:T(8,128)S(1)} %get-tuple-element.14.post, f32[2,80,128]{2,1,0:T(8,128)S(1)} %get-tuple-element.15.zr, f32[2,40,128]{2,1,0:T(8,128)S(1)} %get-tuple-element.16.yr, f32[4,8,128]{2,1,0:T(8,128)S(1)} %get-tuple-element.17.er, ...), custom_call_target="tpu_custom_call" | custom-call | tf_op jit(solution)/shard_map/pallas_call | solution.py:473

commit v5 on v4

--- a/solution.py
+++ b/solution.py
@@ -322,8 +322,9 @@
         )
 
     def each(step, chosen, what):
-        for dz in (0, -1, 1):
-            dirs = [d for d in FAR_FIRST if d in chosen and d[2] == dz]
+        order = FAR_FIRST if what == "start" else FAR_FIRST[::-1]
+        for dz in (0, -1, 1) if what == "start" else (-1, 1, 0):
+            dirs = [d for d in order if d in chosen and d[2] == dz]
             if dirs:
                 def body(dirs=dirs):
                     for d in dirs:
@@ -391,6 +392,10 @@
             early_masks[0]()
         for z in range(Z):
             early[step](z)
+        if step == 1:
+            for sent in range(2):
+                for dirs in (z_dirs, y_dirs, x_dirs):
+                    each(sent, dirs, "wait_send")
         each(step, x_dirs, "wait_recv")
 
     def first_plane(z):
@@ -419,9 +424,6 @@
     cols = columns[0]()
     late_masks[0](cols)
     exchange(1, lambda z: late[0](z, cols))
-    for step in range(2):
-        for dirs in (z_dirs, y_dirs, x_dirs):
-            each(step, dirs, "wait_send")
 
 
 def last(nz, pre, post, zr, yr, er, xr, masks, own_ref, out_hbm, buf, sem):

time: 28.4 us -> 28.4 us (level)
  no operation moved by 1% of the time
where the time goes in v5:
time: 28.4 us; the launch traced here: 28.2 us
  Pallas kernels  28.2 us (99%)
    pallas_call x1, Pallas kernels, shards(): pl.pallas_call(functools.partial(kernel, mesh_shape), out_shape=[jax.Shap...  27.3 us
    pallas_call x1, Pallas kernels, shards(): pl.pallas_call(functools.partial(last, mesh_shape[2]), out_shape=jax.Shap...  0.89 us

profile of v5, /device:TPU:1, one launch (start us, length us, event | category | flops | bytes accessed | tf_op | source)
XLA Modules:
  0.0 28.2 jit_solution(1945067147955910216)
XLA Ops:
  0.0 27.3 %shard_map.46 = (f32[4,27,8,128]{3,2,1,0:T(8,128)S(1)}, f32[4,232,128]{2,1,0:T(8,128)S(1)}, f32[2,80,128]{2,1,0:T(8,128)S(1)}, f32[2,40,128]{2,1,0:T(8,128)S(1)}...) custom-call(f32[27,4,8,128]{3,2,1,0:T(8,128)} %pops_hbm.1, ...), custom_call_target="tpu_custom_call" | custom-call | tf_op jit(solution)/shard_map/pallas_call | solution.py:450
  27.4 0.9 %shard_map.47 = f32[27,4,8,128]{3,2,1,0:T(8,128)} custom-call(f32[4,27,8,128]{3,2,1,0:T(8,128)S(1)} %get-tuple-element.13.pre, f32[4,232,128]{2,1,0:T(8,128)S(1)} %get-tuple-element.14.post, f32[2,80,128]{2,1,0:T(8,128)S(1)} %get-tuple-element.15.zr, f32[2,40,128]{2,1,0:T(8,128)S(1)} %get-tuple-element.16.yr, f32[4,8,128]{2,1,0:T(8,128)S(1)} %get-tuple-element.17.er, ...), custom_call_target="tpu_custom_call" | custom-call | tf_op jit(solution)/shard_map/pallas_call | solution.py:475
